TPU v7x, 128 devices: a whole 4x4x4 slice. The times are simulated.
128 devices in a mesh: atm: 8 (over y, core), ocn: 16 (over x, z).
Axes of the slice: x: 4, y: 4, z: 4, core: 2. Of those that a mesh axis runs over, the one named last changes fastest.
Arguments:
- atm_fields: bfloat16 [65536, 4, 8, 64], P(('atm', 'ocn')), may hold values from -6 to 6
- requests: int32 [128, 128, 6], P(('atm', 'ocn')), may hold values from 0 to 65535, as said below
- ocean_block: int32 [128, 128, 6], P(('atm', 'ocn')), may hold values from 0 to 511
- live_counts: int32 [128, 128], P(('atm', 'ocn')), may hold values from 0 to 6, as said below
- weights: bfloat16 [128, 128, 6, 64, 64], P(('atm', 'ocn')), may hold values from -0.75 to 0.75
Outputs:
- remapped: float32 [65536, 4, 8, 64], P(('atm', 'ocn'))
Inputs may be any that keep to these rules, and one draw needn't show every extreme that they name: requests[d,s,k] names a block of owner s: s*512 <= requests[d,s,k] < (s+1)*512. `live_counts`: every ocean owner has exactly 6 live slots from some source owner.
All inputs are finite; a program needn't handle non-finite values.
Results may differ from a plain program's by a relative error of at most 0.0003.
Values may be sent and summed in bfloat16 or wider, within the bound.
A program may use at most 128 MiB of HBM per device.

v0:
```python
import jax
import jax.numpy as jnp
from jax import lax
from jax.sharding import PartitionSpec as P

OB_DEV = 512


def block_terms(rows, mats, alive):
    part = jnp.einsum("sra,sao->sro", rows, mats, preferred_element_type=jnp.float32)
    return jnp.where(alive[:, None, None], part, jnp.float32(0.0))


def place_blocks(part, targets, nblocks):
    picker = (
        targets[None, :] == lax.broadcasted_iota(jnp.int32, (nblocks, targets.shape[0]), 0)
    ).astype(jnp.float32)
    summed = jnp.dot(
        picker,
        part.reshape(part.shape[0], -1),
        preferred_element_type=jnp.float32,
        precision=lax.Precision.HIGHEST,
    )
    return summed.reshape(nblocks, part.shape[1], part.shape[2])


def on_device(atm_fields, requests, ocean_block, live_counts, weights):
    wanted = requests[0]
    targets = ocean_block[0]
    counts = live_counts[0]
    mats = weights[0]
    owners, cap = wanted.shape
    ab_count = atm_fields.shape[0]
    samples = atm_fields.shape[1]
    fields = atm_fields.shape[2]
    cells = atm_fields.shape[3]
    stacked = samples * fields
    flat_fields = atm_fields.reshape(ab_count, stacked, cells)
    rank = lax.broadcasted_iota(jnp.int32, (owners, cap), 1)
    alive = rank < counts[:, None]
    flat_mats = mats.reshape(owners * cap, cells, cells)
    asked = lax.all_to_all(wanted, ("atm", "ocn"), split_axis=0, concat_axis=0, tiled=True)
    outgoing = jnp.take(flat_fields, (asked % ab_count).reshape(-1), axis=0)
    arrived = lax.all_to_all(
        outgoing.reshape(owners, cap, stacked, cells),
        ("atm", "ocn"),
        split_axis=0,
        concat_axis=0,
        tiled=True,
    )
    arrived = arrived.reshape(owners * cap, stacked, cells)
    whole = block_terms(arrived, flat_mats, alive.reshape(-1))
    total = place_blocks(whole, targets.reshape(-1), OB_DEV)
    return total.reshape(OB_DEV, samples, fields, cells)


def solution(mesh):
    in_specs = (
        P(("atm", "ocn"), None, None, None),
        P(("atm", "ocn"), None, None),
        P(("atm", "ocn"), None, None),
        P(("atm", "ocn"), None),
        P(("atm", "ocn"), None, None, None, None),
    )
    out_specs = P(("atm", "ocn"), None, None, None)
    return jax.shard_map(
        on_device, mesh=mesh, in_specs=in_specs, out_specs=out_specs, check_vma=False
    )
```

profile of v0, /device:TPU:1, one launch (start us, length us, event | category | flops | bytes accessed | tf_op | source)
XLA Modules:
  0.0 136.1 jit_solution(11144032421220522477)
XLA Ops:
  0.0 1.4 %copy.28 = s32[128,1,6]{2,1,0:T(1,128)} copy(s32[128,1,6]{0,1,2:T(1,128)} %bitcast.28) | data formatting | bytes 6144 | tf_op jit(solution)/shard_map/all_to_all | solution.py:42
  1.4 11.5 %all-to-all-start = ((s32[128,1,6]{2,1,0:T(1,128)}), s32[128,1,6]{2,1,0:T(1,128)S(1)}, u32[]{:S(2)}, u32[]{:S(2)}) async-start(s32[128,1,6]{2,1,0:T(1,128)} %copy.28), calls=%async_computation | async-start | bytes 131072 | tf_op jit(solution)/shard_map/all_to_all | solution.py:42
  12.9 7.4 %copy.31 = bf16[512,4,8,64]{3,2,1,0:T(8,128)(2,1)} copy(bf16[512,4,8,64]{0,3,2,1:T(8,128)(2,1)} %param.5) | data formatting | bytes 4194304 | tf_op args[0]
  20.3 2.1 %all-to-all-done = s32[128,1,6]{2,1,0:T(1,128)S(1)} async-done(((s32[128,1,6]{2,1,0:T(1,128)}), s32[128,1,6]{2,1,0:T(1,128)S(1)}, u32[]{:S(2)}, u32[]{:S(2)}) %all-to-all-start) | async-done | bytes 3104 | tf_op jit(solution)/shard_map/all_to_all | solution.py:42
  22.4 0.5 broadcast.108
  22.9 0.7 reduce.5
  23.7 0.1 all_to_all.16
  23.8 0.1 copy.29
  23.9 0.1 copy.30
  24.1 7.2 %gather_fusion = bf16[768,32,64]{2,1,0:T(8,128)(2,1)} fusion(bf16[512,32,64]{2,1,0:T(8,128)(2,1)} %bitcast.26, s32[1024]{0:T(1024)S(1)} %pad_clamp_fusion), kind=kCustom, calls=%fused_computation | custom fusion | bytes 6294528 | tf_op jit(solution)/shard_map/jit(_take)/gather | solution.py:43
  31.3 6.9 %broadcast_select_fusion.1 = bf16[128,6,32,64]{3,2,1,0:T(8,128)(2,1)} fusion(bf16[128,6,32,64]{3,2,1,0:T(8,128)(2,1)} %bitcast.27, pred[128,6]{1,0:T(8,128)(4,1)S(1)} %copy.30), kind=kLoop, calls=%fused_computation.2 | loop fusion | flops 1572864 | bytes 6292224 | tf_op jit(solution)/shard_map/jit(_take)/select_n | solution.py:43
  38.2 10.9 %reshape.124 = bf16[128,2,6144]{2,1,0:T(2,128)(2,1)} reshape(bf16[128,6,32,64]{3,2,1,0:T(8,128)(2,1)} %broadcast_select_fusion.1) | data formatting | bytes 6291456
  49.0 7.7 %all-to-all-start.1 = ((bf16[128,2,6144]{2,1,0:T(2,128)(2,1)}), bf16[128,2,6144]{2,1,0:T(2,128)(2,1)S(1)}, u32[]{:S(2)}, u32[]{:S(2)}) async-start(bf16[128,2,6144]{2,1,0:T(2,128)(2,1)} %reshape.124), calls=%async_computation.1 | async-start | bytes 6291456 | tf_op jit(solution)/shard_map/all_to_all | solution.py:44
  56.7 0.0 copy-start.1
  56.7 0.0 copy-start
  56.7 18.5 %copy.32 = bf16[1,128,6,64,64]{4,3,2,1,0:T(8,128)(2,1)} copy(bf16[1,128,6,64,64]{1,4,3,2,0:T(8,128)(2,1)} %param.9) | data formatting | bytes 12582912 | tf_op args[4]
  75.2 0.0 copy-done.1
  75.2 0.1 iota_compare_fusion.1
  75.3 0.1 lt.46
  75.5 0.0 copy-done
  75.5 0.1 copy.27
  75.6 0.1 eq.12
  75.7 21.9 %all-to-all-done.1 = bf16[128,2,6144]{2,1,0:T(2,128)(2,1)S(1)} async-done(((bf16[128,2,6144]{2,1,0:T(2,128)(2,1)}), bf16[128,2,6144]{2,1,0:T(2,128)(2,1)S(1)}, u32[]{:S(2)}, u32[]{:S(2)}) %all-to-all-start.1) | async-done | bytes 3145760 | tf_op jit(solution)/shard_map/all_to_all | solution.py:44
  97.7 6.2 %reshape.125 = bf16[128,6,32,64]{3,2,1,0:T(8,128)(2,1)} reshape(bf16[128,2,6144]{2,1,0:T(2,128)(2,1)S(1)} %all-to-all-done.1) | data formatting | bytes 6291456
  103.9 10.9 %broadcast_select_fusion = f32[768,32,64]{2,1,0:T(8,128)} fusion(pred[768]{0:T(1024)(128)(4,1)S(1)} %lt.46, bf16[768,32,64]{2,1,0:T(8,128)(2,1)} %bitcast.25, bf16[768,64,64]{2,1,0:T(8,128)(2,1)} %bitcast.23), kind=kOutput, calls=%fused_computation.1 | convolution fusion | flops 202899456 | bytes 15729408 | tf_op jit(solution)/shard_map/sra,sao->sro/dot_general | solution.py:10
  114.7 11.1 %copy.33 = f32[768,32,64]{0,2,1:T(8,128)} copy(f32[768,32,64]{2,1,0:T(8,128)} %broadcast_select_fusion) | data formatting | bytes 12582912 | tf_op jit(solution)/shard_map/jit(_where)/select_n | solution.py:11
  125.8 10.3 %fusion.1 = f32[512,4,8,64]{0,3,2,1:T(8,128)} fusion(f32[4,8,64,768]{3,2,1,0:T(8,128)} %bitcast.24, s32[768]{0:T(1024)S(1)} %eq.12), kind=kOutput, calls=%fused_computation.5 | convolution fusion | flops 9664069632 | bytes 10488832 | tf_op jit(solution)/shard_map/dot_general | solution.py:18
  (3 shorter events, 0.1 us)
Async XLA Ops:
  1.4 21.0 %all-to-all-start = ((s32[128,1,6]{2,1,0:T(1,128)}), s32[128,1,6]{2,1,0:T(1,128)S(1)}, u32[]{:S(2)}, u32[]{:S(2)}) async-start(s32[128,1,6]{2,1,0:T(1,128)} %copy.28), calls=%async_computation | async-start | bytes 131072 | tf_op jit(solution)/shard_map/all_to_all | solution.py:42
  49.0 48.6 %all-to-all-start.1 = ((bf16[128,2,6144]{2,1,0:T(2,128)(2,1)}), bf16[128,2,6144]{2,1,0:T(2,128)(2,1)S(1)}, u32[]{:S(2)}, u32[]{:S(2)}) async-start(bf16[128,2,6144]{2,1,0:T(2,128)(2,1)} %reshape.124), calls=%async_computation.1 | async-start | bytes 6291456 | tf_op jit(solution)/shard_map/all_to_all | solution.py:44
  56.7 18.5 %copy-start.1 = (s32[1,128]{1,0:T(1,128)S(1)}, s32[1,128]{1,0:T(1,128)}, u32[]{:S(2)}) copy-start(s32[1,128]{1,0:T(1,128)} %param.8) | copy-start | bytes 1540
  56.7 18.8 %copy-start = (s32[1,128,6]{1,0,2:T(1,128)S(1)}, s32[1,128,6]{1,0,2:T(1,128)}, u32[]{:S(2)}) copy-start(s32[1,128,6]{1,0,2:T(1,128)} %param.7) | copy-start | bytes 9220
where the time goes:
time: 137 us; the launch traced here: 136 us
  local copies, waits for them, and re-layouts  63.9 us (47%)
  waiting for transfers between devices  24 us (18%)
  matrix products  21.2 us (15%)
  starting transfers between devices  19.2 us (14%)
  other arithmetic  7.75 us (6%)
    unnamed x9, local copies, waits for them, and re-layouts  43.1 us
    all_to_all x1, waiting for transfers between devices, on_device(): lax.all_to_all(outgoing.reshape(owners, cap, stacked, cells), ('atm', 'oc...  21.9 us
    all_to_all x1, starting transfers between devices, on_device(): lax.all_to_all(wanted, ('atm', 'ocn'), split_axis=0, concat_axis=0, tiled...  11.5 us
    select_n x1, local copies, waits for them, and re-layouts, block_terms(): return jnp.where(alive[:, None, None], part, jnp.float32(0.0))  11.1 us
    dot_general x1, matrix products, block_terms(): jnp.einsum('sra,sao->sro', rows, mats, preferred_element_type=jnp.float32)  10.9 us
    dot_general x1, matrix products, place_blocks(): jnp.dot(picker, part.reshape(part.shape[0], -1), preferred_element_type=j...  10.3 us
    all_to_all x1, starting transfers between devices, on_device(): lax.all_to_all(outgoing.reshape(owners, cap, stacked, cells), ('atm', 'oc...  7.66 us
    gather x1, local copies, waits for them, and re-layouts, on_device(): outgoing = jnp.take(flat_fields, (asked % ab_count).reshape(-1), axis=0)  7.2 us
  transfers between devices with their start and end apart: 2, of which 2 were waited for; matrix products, arithmetic and copies ran while one was open for 19% of the time, Pallas kernels for 0%

commit v1 on v0

v1 whole, which is shorter than its diff:
```python
import jax
import jax.numpy as jnp
from jax import lax
from jax.experimental import pallas as pl
from jax.experimental.pallas import tpu as pltpu
from jax.sharding import PartitionSpec as P

MESH = pl.DeviceIdType.MESH
OWNERS = 128
NATM = 8
NOCN = 16
CAP = 6
PAIRS = 3
CELLS = 64
TF = 32
HALF = 16
NBLK = 512
GROUPS = 8
PER = OWNERS // GROUPS
ROWS = PAIRS * TF
WPITCH = CELLS


def shift_of(i):
    j = (i * 37) % OWNERS
    return j // 32, (j // 16) % 2, (j // 4) % 4, j % 4


def moved(i, sign):
    atm = lax.axis_index("atm")
    ocn = lax.axis_index("ocn")
    dy, dc, dx, dz = shift_of(i)
    y = (atm // 2 + 4 + sign * dy) % 4
    c = (atm % 2 + 2 + sign * dc) % 2
    x = (ocn // 4 + 4 + sign * dx) % 4
    z = (ocn % 4 + 4 + sign * dz) % 4
    return y * 2 + c, x * 4 + z


def exchange_kernel(
    x_hbm, req_ref, w_hbm, out_ref,
    xin, win, xt, wt, reqrow, r1, r2, idx, send, recv,
    xsem, wsem, lsem, s1, v1, s2, v2, dsend, drecv,
):
    atm = lax.axis_index("atm")
    ocn = lax.axis_index("ocn")
    xcopy = pltpu.make_async_copy(x_hbm, xin, xsem)
    xcopy.start()
    wcopy = pltpu.make_async_copy(w_hbm, win, wsem)
    wcopy.start()

    barrier = pltpu.get_barrier_semaphore()

    def greet_atm(i, carry):
        pl.semaphore_signal(barrier, inc=1, device_id=((atm + i) % NATM, ocn), device_id_type=MESH)
        return carry

    def greet_ocn(i, carry):
        pl.semaphore_signal(barrier, inc=1, device_id=(atm, (ocn + i) % NOCN), device_id_type=MESH)
        return carry

    lax.fori_loop(1, NATM, greet_atm, 0)
    lax.fori_loop(1, NOCN, greet_ocn, 0)

    padded = jnp.concatenate([req_ref[...] & (NBLK - 1), jnp.zeros((OWNERS - CAP, OWNERS), jnp.int32)], axis=0)
    turned = jnp.transpose(padded)
    for s in range(OWNERS):
        reqrow[s // NOCN, s % NOCN] = turned[s : s + 1, :]

    pl.semaphore_wait(barrier, NATM + NOCN - 2)

    def first_hop(i, carry):
        to = (atm + i) % NATM
        pltpu.make_async_remote_copy(
            reqrow.at[to], r1.at[atm], s1, v1, device_id=(to, ocn), device_id_type=MESH
        ).start()
        return carry

    lax.fori_loop(1, NATM, first_hop, 0)
    own = pltpu.make_async_copy(reqrow.at[atm], r1.at[atm], lsem)
    own.start()

    xcopy.wait()
    xflat = xt.reshape(NBLK * HALF, 2 * CELLS)

    def turn_fields(tp, carry):
        both = jnp.concatenate([xin[tp], xin[tp + HALF]], axis=0).astype(jnp.float32)
        for b in range(0, NBLK, 128):
            xflat[pl.ds(b * HALF + tp, 128, stride=HALF), :] = jnp.transpose(both[:, b : b + 128])
        return carry

    lax.fori_loop(0, HALF // 2, turn_fields, 0)

    own.wait()
    hop1 = pltpu.make_async_remote_copy(
        reqrow.at[pl.ds(0, NATM - 1)], r1.at[pl.ds(0, NATM - 1)], s1, v1,
        device_id=(atm, ocn), device_id_type=MESH,
    )
    hop1.wait_recv()

    def second_hop(i, carry):
        to = (ocn + i) % NOCN
        pltpu.make_async_remote_copy(
            r1.at[:, to], r2.at[ocn], s2, v2, device_id=(atm, to), device_id_type=MESH
        ).start()
        return carry

    lax.fori_loop(1, NOCN, second_hop, 0)
    own2 = pltpu.make_async_copy(r1.at[:, ocn], r2.at[ocn], lsem)
    own2.start()

    lax.fori_loop(HALF // 2, HALF, turn_fields, 0)

    own2.wait()
    hop1.wait_send()
    hop2 = pltpu.make_async_remote_copy(
        r2.at[pl.ds(0, NOCN - 1)], r2.at[pl.ds(0, NOCN - 1)], s2, v2,
        device_id=(atm, ocn), device_id_type=MESH,
    )
    hop2.wait_recv()
    hop2.wait_send()
    tosmem = pltpu.make_async_copy(r2, idx, lsem)
    tosmem.start()
    tosmem.wait()

    left = lax.broadcasted_iota(jnp.int32, (HALF, 2 * CELLS), 1) < CELLS

    def fill(i, box, at):
        ta, to = moved(i, 1)
        for p in range(PAIRS):
            ia = idx[to, ta, 0, 2 * p]
            ib = idx[to, ta, 0, 2 * p + 1]
            a = xt[ia]
            b = xt[ib]
            low = jnp.where(left, a, pltpu.roll(b, CELLS, 1))
            high = jnp.where(left, pltpu.roll(a, CELLS, 1), b)
            box[at, p * TF : p * TF + HALF, :] = low.astype(jnp.bfloat16)
            box[at, p * TF + HALF : (p + 1) * TF, :] = high.astype(jnp.bfloat16)
        return ta, to

    fill(0, recv, 0)

    def ship(i, carry):
        ta, to = fill(i, send, i)
        pltpu.make_async_remote_copy(
            send.at[i], recv.at[i], dsend, drecv.at[i // PER],
            device_id=(ta, to), device_id_type=MESH,
        ).start()
        return carry

    lax.fori_loop(1, OWNERS, ship, 0)

    wcopy.wait()
    for p in range(PAIRS):
        def turn_weights(a, carry):
            both = jnp.concatenate([win[2 * p, a], win[2 * p + 1, a]], axis=0).astype(jnp.float32)
            wt[p, pl.ds(a, OWNERS, stride=WPITCH), :] = jnp.transpose(both)
            return carry

        lax.fori_loop(0, CELLS, turn_weights, 0)

    lane = lax.broadcasted_iota(jnp.int32, (CELLS, 2 * CELLS), 1) < CELLS

    def apply(i, carry):
        fa, fo = moved(i, -1)
        s = fa * NOCN + fo
        for p in range(PAIRS):
            w = wt[p, pl.ds(pl.multiple_of(s * WPITCH, 8), CELLS), :]
            zero = jnp.zeros_like(w)
            square = jnp.concatenate([jnp.where(lane, w, zero), jnp.where(lane, zero, w)], axis=0).astype(jnp.bfloat16)
            part = jnp.dot(recv[i, p * TF : (p + 1) * TF, :], square, preferred_element_type=jnp.float32)
            out_ref[pl.ds(p * OWNERS + s, TF, stride=PAIRS * OWNERS), :] = part
        return carry

    for g in range(GROUPS):
        n = PER - 1 if g == 0 else PER
        pltpu.make_async_remote_copy(
            send.at[pl.ds(0, n)], recv.at[pl.ds(0, n)], dsend, drecv.at[g],
            device_id=(atm, ocn), device_id_type=MESH,
        ).wait_recv()
        lax.fori_loop(g * PER, (g + 1) * PER, apply, 0)

    pltpu.make_async_remote_copy(
        send.at[pl.ds(1, OWNERS - 1)], recv.at[pl.ds(1, OWNERS - 1)], dsend, drecv.at[0],
        device_id=(atm, ocn), device_id_type=MESH,
    ).wait_send()


def exchange(fields, req, mats):
    big = pl.BlockSpec(memory_space=pl.ANY)
    vmem = pl.BlockSpec(memory_space=pltpu.VMEM)
    return pl.pallas_call(
        exchange_kernel,
        out_shape=jax.ShapeDtypeStruct((TF * PAIRS * OWNERS, 2 * CELLS), jnp.float32),
        in_specs=[big, vmem, big],
        out_specs=vmem,
        scratch_shapes=[
            pltpu.VMEM((TF, CELLS, NBLK), jnp.bfloat16),
            pltpu.VMEM((CAP, CELLS, CELLS, OWNERS), jnp.bfloat16),
            pltpu.VMEM((NBLK, HALF, 2 * CELLS), jnp.float32),
            pltpu.VMEM((PAIRS, OWNERS * WPITCH, 2 * CELLS), jnp.float32),
            pltpu.VMEM((NATM, NOCN, 1, 128), jnp.int32),
            pltpu.VMEM((NATM, NOCN, 1, 128), jnp.int32),
            pltpu.VMEM((NOCN, NATM, 1, 128), jnp.int32),
            pltpu.SMEM((NOCN, NATM, 1, 128), jnp.int32),
            pltpu.VMEM((OWNERS, ROWS, 2 * CELLS), jnp.bfloat16),
            pltpu.VMEM((OWNERS, ROWS, 2 * CELLS), jnp.bfloat16),
            pltpu.SemaphoreType.DMA,
            pltpu.SemaphoreType.DMA,
            pltpu.SemaphoreType.DMA,
            pltpu.SemaphoreType.DMA,
            pltpu.SemaphoreType.DMA,
            pltpu.SemaphoreType.DMA,
            pltpu.SemaphoreType.DMA,
            pltpu.SemaphoreType.DMA,
            pltpu.SemaphoreType.DMA((GROUPS,)),
        ],
        compiler_params=pltpu.CompilerParams(
            collective_id=0, has_side_effects=True, vmem_limit_bytes=56 << 20
        ),
        name="exchange",
    )(fields, req, mats)


def place_kernel(p_ref, tgt_ref, cnt_ref, o_ref, hot, lhs):
    @pl.when(pl.program_id(0) == 0)
    def _():
        block = lax.broadcasted_iota(jnp.int32, (NBLK, OWNERS), 0)
        for par in range(2):
            for p in range(PAIRS):
                k = 2 * p + par
                live = jnp.where(cnt_ref[...] > k, tgt_ref[k : k + 1, :], -1)
                at = (par * PAIRS + p) * OWNERS
                hot[:, at : at + OWNERS] = jnp.where(block == live, 1.0, 0.0).astype(jnp.bfloat16)

    nf = p_ref.shape[0]
    for f in range(nf):
        turned = jnp.transpose(p_ref[f])
        rows = jnp.concatenate([turned[:CELLS], turned[CELLS:]], axis=1)
        high = rows.astype(jnp.bfloat16)
        low = (rows - high.astype(jnp.float32)).astype(jnp.bfloat16)
        lhs[f * CELLS : (f + 1) * CELLS, :] = high
        lhs[(nf + f) * CELLS : (nf + f + 1) * CELLS, :] = low
    both = lax.dot_general(
        lhs[...], hot[...], (((1,), (1,)), ((), ())), preferred_element_type=jnp.float32
    )
    total = both[: nf * CELLS] + both[nf * CELLS :]
    o_ref[...] = total.reshape(nf, CELLS, NBLK)


def place(parts, targets, counts):
    nf = 8
    return pl.pallas_call(
        place_kernel,
        grid=(TF // nf,),
        out_shape=jax.ShapeDtypeStruct((TF, CELLS, NBLK), jnp.float32),
        in_specs=[
            pl.BlockSpec((nf, PAIRS * OWNERS, 2 * CELLS), lambda t: (t, 0, 0)),
            pl.BlockSpec((CAP, OWNERS), lambda t: (0, 0)),
            pl.BlockSpec((1, OWNERS), lambda t: (0, 0)),
        ],
        out_specs=pl.BlockSpec((nf, CELLS, NBLK), lambda t: (t, 0, 0)),
        scratch_shapes=[
            pltpu.VMEM((NBLK, 2 * PAIRS * OWNERS), jnp.bfloat16),
            pltpu.VMEM((2 * nf * CELLS, 2 * PAIRS * OWNERS), jnp.bfloat16),
        ],
        compiler_params=pltpu.CompilerParams(vmem_limit_bytes=48 << 20),
        name="place",
    )(parts, targets, counts)


def on_device(atm_fields, requests, ocean_block, live_counts, weights):
    fields = jnp.transpose(atm_fields, (1, 2, 3, 0)).reshape(TF, CELLS, NBLK)
    req = jnp.transpose(requests[0])
    targets = jnp.transpose(ocean_block[0])
    mats = jnp.transpose(weights[0], (1, 2, 3, 0))
    parts = exchange(fields, req, mats)
    out = place(parts.reshape(TF, PAIRS * OWNERS, 2 * CELLS), targets, live_counts)
    return jnp.transpose(out.reshape(4, 8, CELLS, NBLK), (3, 0, 1, 2))


def solution(mesh):
    in_specs = (
        P(("atm", "ocn"), None, None, None),
        P(("atm", "ocn"), None, None),
        P(("atm", "ocn"), None, None),
        P(("atm", "ocn"), None),
        P(("atm", "ocn"), None, None, None, None),
    )
    out_specs = P(("atm", "ocn"), None, None, None)
    return jax.shard_map(
        on_device, mesh=mesh, in_specs=in_specs, out_specs=out_specs, check_vma=False
    )
```

time: 137 us -> 92.9 us (0.68)
  Pallas kernels: 0 us -> 90.7 us
  local copies, waits for them, and re-layouts: 63.9 us -> 1.96 us
  waiting for transfers between devices: 24 us -> 0 us
  matrix products: 21.2 us -> 0 us
  starting transfers between devices: 19.2 us -> 0 us
  other arithmetic: 7.75 us -> 0 us
    pallas_call x0 -> x2, Pallas kernels: none -> 90.7 us  [the longest x1 82.5 us: exchange(): pl.pallas_call(exchange_kernel, out_shape=jax.ShapeDtypeStruct((TF * PAIR...]
    unnamed x9 -> x4, local copies, waits for them, and re-layouts: 43.1 us -> 1.96 us
    all_to_all x2 -> x0, waiting for transfers between devices: 24 us -> none  [the longest x1 21.9 us: on_device(): lax.all_to_all(outgoing.reshape(owners, cap, stacked, cells), ('atm', 'oc...]
    dot_general x2 -> x0, matrix products: 21.2 us -> none  [the longest x1 10.9 us: block_terms(): jnp.einsum('sra,sao->sro', rows, mats, preferred_element_type=jnp.float32)]
    all_to_all x2 -> x0, starting transfers between devices: 19.2 us -> none  [the longest x1 11.5 us: on_device(): lax.all_to_all(wanted, ('atm', 'ocn'), split_axis=0, concat_axis=0, tiled...]
    select_n x1 -> x0, local copies, waits for them, and re-layouts: 11.1 us -> none  [block_terms(): return jnp.where(alive[:, None, None], part, jnp.float32(0.0))]
    gather x1 -> x0, local copies, waits for them, and re-layouts: 7.2 us -> none  [on_device(): outgoing = jnp.take(flat_fields, (asked % ab_count).reshape(-1), axis=0)]
    select_n x2 -> x0, other arithmetic: 6.92 us -> none  [on_device(): outgoing = jnp.take(flat_fields, (asked % ab_count).reshape(-1), axis=0)]
  transfers between devices with their start and end apart: 2 -> 0, of which waited for: 2 -> 0; matrix products, arithmetic and copies ran while one was open for 19% -> 0% of each run, Pallas kernels for 0% -> 0%
where the time goes in v1:
time: 92.9 us; the launch traced here: 92.7 us
  Pallas kernels  90.7 us (98%)
  local copies, waits for them, and re-layouts  1.96 us (2%)
    pallas_call x1, Pallas kernels, exchange(): pl.pallas_call(exchange_kernel, out_shape=jax.ShapeDtypeStruct((TF * PAIR...  82.5 us
    pallas_call x1, Pallas kernels, place(): pl.pallas_call(place_kernel, grid=(TF // nf,), out_shape=jax.ShapeDtypeSt...  8.17 us
    unnamed x4, local copies, waits for them, and re-layouts  1.96 us

profile of v1, /device:TPU:1, one launch (start us, length us, event | category | flops | bytes accessed | tf_op | source)
XLA Modules:
  0.0 92.7 jit_solution(4510934966120506273)
XLA Ops:
  0.0 1.3 %copy.11 = s32[1,128,6]{1,2,0:T(8,128)} copy(s32[1,128,6]{1,0,2:T(1,128)} %param.6) | data formatting | bytes 6144
  1.3 0.7 copy.10
  2.0 0.0 copy-start
  2.0 82.5 %exchange.1 = f32[12288,128]{1,0:T(8,128)} custom-call(bf16[32,64,512]{2,1,0:T(8,128)(2,1)} %bitcast.23, s32[6,128]{1,0:T(8,128)} %bitcast.24, bf16[6,64,64,128]{3,2,1,0:T(8,128)(2,1)} %bitcast.22), custom_call_target="tpu_custom_call" | custom-call | tf_op jit(solution)/shard_map/exchange/pallas_call | solution.py:192
  84.5 0.0 copy-done
  84.5 8.2 %place.1 = f32[32,64,512]{2,1,0:T(8,128)} custom-call(f32[32,384,128]{2,1,0:T(8,128)} %bitcast.21, s32[6,128]{1,0:T(8,128)S(1)} %bitcast.20, s32[1,128]{1,0:T(1,128)S(1)} %copy-done), custom_call_target="tpu_custom_call" | custom-call | tf_op jit(solution)/shard_map/place/pallas_call | solution.py:253
Async XLA Ops:
  2.0 82.5 %copy-start = (s32[1,128]{1,0:T(1,128)S(1)}, s32[1,128]{1,0:T(1,128)}, u32[]{:S(2)}) copy-start(s32[1,128]{1,0:T(1,128)} %cnt_ref.1) | copy-start | bytes 1540

commit v2 on v1

--- a/solution.py
+++ b/solution.py
@@ -10,12 +10,13 @@
 NATM = 8
 NOCN = 16
 CAP = 6
+KROWS = 8
 PAIRS = 3
 CELLS = 64
 TF = 32
 HALF = 16
 NBLK = 512
-GROUPS = 8
+GROUPS = 16
 PER = OWNERS // GROUPS
 ROWS = PAIRS * TF
 WPITCH = CELLS
@@ -39,7 +40,7 @@
 
 def exchange_kernel(
     x_hbm, req_ref, w_hbm, out_ref,
-    xin, win, xt, wt, reqrow, r1, r2, idx, send, recv,
+    xin, win, xt, wt, reqm, r1, turned, rows, r2, idx, send, recv,
     xsem, wsem, lsem, s1, v1, s2, v2, dsend, drecv,
 ):
     atm = lax.axis_index("atm")
@@ -62,23 +63,20 @@
     lax.fori_loop(1, NATM, greet_atm, 0)
     lax.fori_loop(1, NOCN, greet_ocn, 0)
 
-    padded = jnp.concatenate([req_ref[...] & (NBLK - 1), jnp.zeros((OWNERS - CAP, OWNERS), jnp.int32)], axis=0)
-    turned = jnp.transpose(padded)
-    for s in range(OWNERS):
-        reqrow[s // NOCN, s % NOCN] = turned[s : s + 1, :]
+    for k in range(CAP):
+        reqm[k : k + 1, :] = req_ref[k] & (NBLK - 1)
+    reqm[CAP:, :] = jnp.zeros((KROWS - CAP, OWNERS), jnp.int32)
 
     pl.semaphore_wait(barrier, NATM + NOCN - 2)
 
     def first_hop(i, carry):
-        to = (atm + i) % NATM
         pltpu.make_async_remote_copy(
-            reqrow.at[to], r1.at[atm], s1, v1, device_id=(to, ocn), device_id_type=MESH
+            reqm, r1.at[atm], s1, v1, device_id=((atm + i) % NATM, ocn), device_id_type=MESH
         ).start()
         return carry
 
     lax.fori_loop(1, NATM, first_hop, 0)
-    own = pltpu.make_async_copy(reqrow.at[atm], r1.at[atm], lsem)
-    own.start()
+    r1[atm] = reqm[...]
 
     xcopy.wait()
     xflat = xt.reshape(NBLK * HALF, 2 * CELLS)
@@ -91,27 +89,29 @@
 
     lax.fori_loop(0, HALF // 2, turn_fields, 0)
 
-    own.wait()
     hop1 = pltpu.make_async_remote_copy(
-        reqrow.at[pl.ds(0, NATM - 1)], r1.at[pl.ds(0, NATM - 1)], s1, v1,
+        r1.at[pl.ds(0, NATM - 1)], r1.at[pl.ds(0, NATM - 1)], s1, v1,
         device_id=(atm, ocn), device_id_type=MESH,
     )
     hop1.wait_recv()
+    half = r1[...].reshape(NATM * KROWS, OWNERS)
+    turned[...] = jnp.transpose(jnp.concatenate([half, half], axis=0))
+    mine = turned[pl.ds(pl.multiple_of(atm * NOCN, NOCN), NOCN), :]
+    for o in range(NOCN):
+        rows[o] = mine[o : o + 1, :]
 
     def second_hop(i, carry):
         to = (ocn + i) % NOCN
         pltpu.make_async_remote_copy(
-            r1.at[:, to], r2.at[ocn], s2, v2, device_id=(atm, to), device_id_type=MESH
+            rows.at[to], r2.at[ocn], s2, v2, device_id=(atm, to), device_id_type=MESH
         ).start()
         return carry
 
     lax.fori_loop(1, NOCN, second_hop, 0)
-    own2 = pltpu.make_async_copy(r1.at[:, ocn], r2.at[ocn], lsem)
-    own2.start()
+    r2[ocn] = rows[ocn]
 
     lax.fori_loop(HALF // 2, HALF, turn_fields, 0)
 
-    own2.wait()
     hop1.wait_send()
     hop2 = pltpu.make_async_remote_copy(
         r2.at[pl.ds(0, NOCN - 1)], r2.at[pl.ds(0, NOCN - 1)], s2, v2,
@@ -128,8 +128,8 @@
     def fill(i, box, at):
         ta, to = moved(i, 1)
         for p in range(PAIRS):
-            ia = idx[to, ta, 0, 2 * p]
-            ib = idx[to, ta, 0, 2 * p + 1]
+            ia = idx[to, 0, ta * KROWS + 2 * p]
+            ib = idx[to, 0, ta * KROWS + 2 * p + 1]
             a = xt[ia]
             b = xt[ib]
             low = jnp.where(left, a, pltpu.roll(b, CELLS, 1))
@@ -148,7 +148,15 @@
         ).start()
         return carry
 
-    lax.fori_loop(1, OWNERS, ship, 0)
+    for i in range(1, 4):
+        ship(i, 0)
+
+    def ship_four(q, carry):
+        for i in range(4):
+            ship(4 * q + i, 0)
+        return carry
+
+    lax.fori_loop(1, OWNERS // 4, ship_four, 0)
 
     wcopy.wait()
     for p in range(PAIRS):
@@ -157,7 +165,7 @@
             wt[p, pl.ds(a, OWNERS, stride=WPITCH), :] = jnp.transpose(both)
             return carry
 
-        lax.fori_loop(0, CELLS, turn_weights, 0)
+        lax.fori_loop(0, CELLS, turn_weights, 0, unroll=8)
 
     lane = lax.broadcasted_iota(jnp.int32, (CELLS, 2 * CELLS), 1) < CELLS
 
@@ -166,8 +174,9 @@
         s = fa * NOCN + fo
         for p in range(PAIRS):
             w = wt[p, pl.ds(pl.multiple_of(s * WPITCH, 8), CELLS), :]
+            w = w.astype(jnp.bfloat16)
             zero = jnp.zeros_like(w)
-            square = jnp.concatenate([jnp.where(lane, w, zero), jnp.where(lane, zero, w)], axis=0).astype(jnp.bfloat16)
+            square = jnp.concatenate([jnp.where(lane, w, zero), jnp.where(lane, zero, w)], axis=0)
             part = jnp.dot(recv[i, p * TF : (p + 1) * TF, :], square, preferred_element_type=jnp.float32)
             out_ref[pl.ds(p * OWNERS + s, TF, stride=PAIRS * OWNERS), :] = part
         return carry
@@ -178,7 +187,7 @@
             send.at[pl.ds(0, n)], recv.at[pl.ds(0, n)], dsend, drecv.at[g],
             device_id=(atm, ocn), device_id_type=MESH,
         ).wait_recv()
-        lax.fori_loop(g * PER, (g + 1) * PER, apply, 0)
+        lax.fori_loop(g * PER, (g + 1) * PER, apply, 0, unroll=4)
 
     pltpu.make_async_remote_copy(
         send.at[pl.ds(1, OWNERS - 1)], recv.at[pl.ds(1, OWNERS - 1)], dsend, drecv.at[0],
@@ -199,10 +208,12 @@
             pltpu.VMEM((CAP, CELLS, CELLS, OWNERS), jnp.bfloat16),
             pltpu.VMEM((NBLK, HALF, 2 * CELLS), jnp.float32),
             pltpu.VMEM((PAIRS, OWNERS * WPITCH, 2 * CELLS), jnp.float32),
-            pltpu.VMEM((NATM, NOCN, 1, 128), jnp.int32),
-            pltpu.VMEM((NATM, NOCN, 1, 128), jnp.int32),
-            pltpu.VMEM((NOCN, NATM, 1, 128), jnp.int32),
-            pltpu.SMEM((NOCN, NATM, 1, 128), jnp.int32),
+            pltpu.VMEM((KROWS, OWNERS), jnp.int32),
+            pltpu.VMEM((NATM, KROWS, OWNERS), jnp.int32),
+            pltpu.VMEM((OWNERS, OWNERS), jnp.int32),
+            pltpu.VMEM((NOCN, 1, OWNERS), jnp.int32),
+            pltpu.VMEM((NOCN, 1, OWNERS), jnp.int32),
+            pltpu.SMEM((NOCN, 1, OWNERS), jnp.int32),
             pltpu.VMEM((OWNERS, ROWS, 2 * CELLS), jnp.bfloat16),
             pltpu.VMEM((OWNERS, ROWS, 2 * CELLS), jnp.bfloat16),
             pltpu.SemaphoreType.DMA,
@@ -229,7 +240,7 @@
         for par in range(2):
             for p in range(PAIRS):
                 k = 2 * p + par
-                live = jnp.where(cnt_ref[...] > k, tgt_ref[k : k + 1, :], -1)
+                live = jnp.where(cnt_ref[...] > k, tgt_ref[k], -1)
                 at = (par * PAIRS + p) * OWNERS
                 hot[:, at : at + OWNERS] = jnp.where(block == live, 1.0, 0.0).astype(jnp.bfloat16)
 
@@ -256,7 +267,7 @@
         out_shape=jax.ShapeDtypeStruct((TF, CELLS, NBLK), jnp.float32),
         in_specs=[
             pl.BlockSpec((nf, PAIRS * OWNERS, 2 * CELLS), lambda t: (t, 0, 0)),
-            pl.BlockSpec((CAP, OWNERS), lambda t: (0, 0)),
+            pl.BlockSpec((CAP, 1, OWNERS), lambda t: (0, 0, 0)),
             pl.BlockSpec((1, OWNERS), lambda t: (0, 0)),
         ],
         out_specs=pl.BlockSpec((nf, CELLS, NBLK), lambda t: (t, 0, 0)),
@@ -271,8 +282,8 @@
 
 def on_device(atm_fields, requests, ocean_block, live_counts, weights):
     fields = jnp.transpose(atm_fields, (1, 2, 3, 0)).reshape(TF, CELLS, NBLK)
-    req = jnp.transpose(requests[0])
-    targets = jnp.transpose(ocean_block[0])
+    req = jnp.transpose(requests, (2, 0, 1))
+    targets = jnp.transpose(ocean_block, (2, 0, 1))
     mats = jnp.transpose(weights[0], (1, 2, 3, 0))
     parts = exchange(fields, req, mats)
     out = place(parts.reshape(TF, PAIRS * OWNERS, 2 * CELLS), targets, live_counts)

time: 92.9 us -> 69.4 us (0.75)
  the two profiles are of different devices: /device:TPU:1 before, /device:TPU:8 now
where the time goes in v2:
time: 69.4 us; the launch traced here: 69.2 us
  Pallas kernels  69.2 us (100%)
    pallas_call x1, Pallas kernels, exchange(): pl.pallas_call(exchange_kernel, out_shape=jax.ShapeDtypeStruct((TF * PAIR...  61 us
    pallas_call x1, Pallas kernels, place(): pl.pallas_call(place_kernel, grid=(TF // nf,), out_shape=jax.ShapeDtypeSt...  8.17 us

profile of v2, /device:TPU:8, one launch (start us, length us, event | category | flops | bytes accessed | tf_op | source)
XLA Modules:
  0.0 69.2 jit_solution(5583058259237011303)
XLA Ops:
  0.0 0.0 copy-start
  0.0 0.0 copy-start.1
  0.0 61.0 %exchange.1 = f32[12288,128]{1,0:T(8,128)} custom-call(bf16[32,64,512]{2,1,0:T(8,128)(2,1)} %bitcast.15, s32[6,1,128]{2,1,0:T(1,128)} %bitcast.16, bf16[6,64,64,128]{3,2,1,0:T(8,128)(2,1)} %bitcast.14), custom_call_target="tpu_custom_call" | custom-call | tf_op jit(solution)/shard_map/exchange/pallas_call | solution.py:201
  61.0 0.0 copy-done
  61.0 0.0 copy-done.1
  61.1 8.2 %place.1 = f32[32,64,512]{2,1,0:T(8,128)} custom-call(f32[32,384,128]{2,1,0:T(8,128)} %bitcast.13, s32[6,1,128]{2,1,0:T(1,128)S(1)} %bitcast.12, s32[1,128]{1,0:T(1,128)S(1)} %copy-done.1), custom_call_target="tpu_custom_call" | custom-call | tf_op jit(solution)/shard_map/place/pallas_call | solution.py:264
Async XLA Ops:
  0.0 61.0 %copy-start = (s32[1,128,6]{1,0,2:T(1,128)S(1)}, s32[1,128,6]{1,0,2:T(1,128)}, u32[]{:S(2)}) copy-start(s32[1,128,6]{1,0,2:T(1,128)} %param.7) | copy-start | bytes 9220
  0.0 61.0 %copy-start.1 = (s32[1,128]{1,0:T(1,128)S(1)}, s32[1,128]{1,0:T(1,128)}, u32[]{:S(2)}) copy-start(s32[1,128]{1,0:T(1,128)} %cnt_ref.1) | copy-start | bytes 1540

commit v3 on v2

--- a/solution.py
+++ b/solution.py
@@ -17,6 +17,7 @@
 HALF = 16
 NBLK = 512
 GROUPS = 16
+TFS = 16
 PER = OWNERS // GROUPS
 ROWS = PAIRS * TF
 WPITCH = CELLS
@@ -38,13 +39,30 @@
     return y * 2 + c, x * 4 + z
 
 
+def sender_of(i):
+    atm = lax.axis_index("atm")
+    ocn = lax.axis_index("ocn")
+    j = (i * 37) & (OWNERS - 1)
+    y = (atm // 2 - (j >> 5)) & 3
+    c = (atm % 2 - (j >> 4)) & 1
+    x = (ocn // 4 - (j >> 2)) & 3
+    z = (ocn % 4 - j) & 3
+    return ((y * 2 + c) * 4 + x) * 4 + z
+
+
 def exchange_kernel(
-    x_hbm, req_ref, w_hbm, out_ref,
-    xin, win, xt, wt, reqm, r1, turned, rows, r2, idx, send, recv,
-    xsem, wsem, lsem, s1, v1, s2, v2, dsend, drecv,
+    x_hbm, req_hbm, w_hbm, tgt_hbm, cnt_hbm, acc,
+    req_ref, tgt_ref, cnt_ref, xin, win, xt, wt, reqm, r1, turned, rows, r2, idx, send, recv, part, lhs, hot,
+    xsem, wsem, lsem, isem, s1, v1, s2, v2, dsend, drecv,
 ):
     atm = lax.axis_index("atm")
     ocn = lax.axis_index("ocn")
+    small = [
+        pltpu.make_async_copy(a, b, isem.at[n])
+        for n, (a, b) in enumerate(((req_hbm, req_ref), (tgt_hbm, tgt_ref), (cnt_hbm, cnt_ref)))
+    ]
+    for copy in small:
+        copy.start()
     xcopy = pltpu.make_async_copy(x_hbm, xin, xsem)
     xcopy.start()
     wcopy = pltpu.make_async_copy(w_hbm, win, wsem)
@@ -52,30 +70,21 @@
 
     barrier = pltpu.get_barrier_semaphore()
 
-    def greet_atm(i, carry):
+    for i in range(1, NATM):
         pl.semaphore_signal(barrier, inc=1, device_id=((atm + i) % NATM, ocn), device_id_type=MESH)
-        return carry
-
-    def greet_ocn(i, carry):
+    for i in range(1, NOCN):
         pl.semaphore_signal(barrier, inc=1, device_id=(atm, (ocn + i) % NOCN), device_id_type=MESH)
-        return carry
-
-    lax.fori_loop(1, NATM, greet_atm, 0)
-    lax.fori_loop(1, NOCN, greet_ocn, 0)
-
+    small[0].wait()
     for k in range(CAP):
         reqm[k : k + 1, :] = req_ref[k] & (NBLK - 1)
     reqm[CAP:, :] = jnp.zeros((KROWS - CAP, OWNERS), jnp.int32)
 
     pl.semaphore_wait(barrier, NATM + NOCN - 2)
 
-    def first_hop(i, carry):
+    for i in range(1, NATM):
         pltpu.make_async_remote_copy(
             reqm, r1.at[atm], s1, v1, device_id=((atm + i) % NATM, ocn), device_id_type=MESH
         ).start()
-        return carry
-
-    lax.fori_loop(1, NATM, first_hop, 0)
     r1[atm] = reqm[...]
 
     xcopy.wait()
@@ -100,14 +109,11 @@
     for o in range(NOCN):
         rows[o] = mine[o : o + 1, :]
 
-    def second_hop(i, carry):
+    for i in range(1, NOCN):
         to = (ocn + i) % NOCN
         pltpu.make_async_remote_copy(
             rows.at[to], r2.at[ocn], s2, v2, device_id=(atm, to), device_id_type=MESH
         ).start()
-        return carry
-
-    lax.fori_loop(1, NOCN, second_hop, 0)
     r2[ocn] = rows[ocn]
 
     lax.fori_loop(HALF // 2, HALF, turn_fields, 0)
@@ -167,6 +173,35 @@
 
         lax.fori_loop(0, CELLS, turn_weights, 0, unroll=8)
 
+    small[1].wait()
+    small[2].wait()
+    j = lax.broadcasted_iota(jnp.int32, (PAIRS * OWNERS, OWNERS), 0)
+    step = (j * 171) >> 9
+    pair = j - PAIRS * step
+    came = sender_of(step)
+    col = lax.broadcasted_iota(jnp.int32, (PAIRS * OWNERS, OWNERS), 1)
+    found = jnp.zeros((PAIRS * OWNERS, KROWS), jnp.float32)
+    for p in range(PAIRS):
+        pick = jnp.where((came == col) & (pair == p), 1.0, 0.0).astype(jnp.bfloat16)
+        terms = []
+        for par in range(2):
+            k = 2 * p + par
+            goal = jnp.where(cnt_ref[...] > k, tgt_ref[k] + 1, 0)
+            terms += [goal >> 4, goal & 15]
+        terms = jnp.concatenate(terms + terms, axis=0).astype(jnp.float32).astype(jnp.bfloat16)
+        found += lax.dot_general(
+            pick, terms, (((1,), (1,)), ((), ())), preferred_element_type=jnp.float32
+        )
+    block = lax.broadcasted_iota(jnp.int32, (OWNERS, NBLK), 1).astype(jnp.float32)
+    for par in range(2):
+        goal = found[:, 2 * par : 2 * par + 1] * 16.0 + found[:, 2 * par + 1 : 2 * par + 2] - 1.0
+        for b in range(PAIRS):
+            mine = goal[b * OWNERS : (b + 1) * OWNERS]
+            ones = jnp.where(block == mine, 1.0, 0.0).astype(jnp.bfloat16)
+            for h in range(2):
+                at = (2 * h + par) * OWNERS
+                hot[b, at : at + OWNERS, :] = ones
+
     lane = lax.broadcasted_iota(jnp.int32, (CELLS, 2 * CELLS), 1) < CELLS
 
     def apply(i, carry):
@@ -177,9 +212,26 @@
             w = w.astype(jnp.bfloat16)
             zero = jnp.zeros_like(w)
             square = jnp.concatenate([jnp.where(lane, w, zero), jnp.where(lane, zero, w)], axis=0)
-            part = jnp.dot(recv[i, p * TF : (p + 1) * TF, :], square, preferred_element_type=jnp.float32)
-            out_ref[pl.ds(p * OWNERS + s, TF, stride=PAIRS * OWNERS), :] = part
+            prod = jnp.dot(recv[i, p * TF : (p + 1) * TF, :], square, preferred_element_type=jnp.float32)
+            part[pl.ds(PAIRS * i + p, TF, stride=PAIRS * OWNERS), :] = prod
         return carry
+
+    def turn_parts(b, tf):
+        rows = part[pl.ds(pl.multiple_of(tf * PAIRS * OWNERS + b * OWNERS, OWNERS), OWNERS), :]
+        rows = jnp.transpose(rows)
+        high = rows.astype(jnp.bfloat16)
+        low = (rows - high.astype(jnp.float32)).astype(jnp.bfloat16)
+        at = pl.ds(pl.multiple_of(tf * CELLS, CELLS), CELLS)
+        for h, term in enumerate((high, low)):
+            lhs[at, 2 * h * OWNERS : (2 * h + 1) * OWNERS] = term[:CELLS]
+            lhs[at, (2 * h + 1) * OWNERS : (2 * h + 2) * OWNERS] = term[CELLS:]
+
+    def place(b, tf):
+        at = pl.ds(pl.multiple_of(tf * CELLS, CELLS), TFS * CELLS)
+        more = jnp.dot(lhs[at, :], hot[b], preferred_element_type=jnp.float32)
+        if b:
+            more += acc[at, :]
+        acc[at, :] = more
 
     for g in range(GROUPS):
         n = PER - 1 if g == 0 else PER
@@ -188,6 +240,15 @@
             device_id=(atm, ocn), device_id_type=MESH,
         ).wait_recv()
         lax.fori_loop(g * PER, (g + 1) * PER, apply, 0, unroll=4)
+        for b in range(PAIRS):
+            if g * PER * PAIRS < (b + 1) * OWNERS <= (g + 1) * PER * PAIRS:
+                def some(q, carry):
+                    for t in range(TFS):
+                        turn_parts(b, q * TFS + t)
+                    place(b, q * TFS)
+                    return carry
+
+                lax.fori_loop(0, TF // TFS, some, 0)
 
     pltpu.make_async_remote_copy(
         send.at[pl.ds(1, OWNERS - 1)], recv.at[pl.ds(1, OWNERS - 1)], dsend, drecv.at[0],
@@ -195,15 +256,17 @@
     ).wait_send()
 
 
-def exchange(fields, req, mats):
-    big = pl.BlockSpec(memory_space=pl.ANY)
-    vmem = pl.BlockSpec(memory_space=pltpu.VMEM)
+def exchange(fields, req, mats, targets, counts):
+    far = pl.BlockSpec(memory_space=pltpu.HBM)
     return pl.pallas_call(
         exchange_kernel,
-        out_shape=jax.ShapeDtypeStruct((TF * PAIRS * OWNERS, 2 * CELLS), jnp.float32),
-        in_specs=[big, vmem, big],
-        out_specs=vmem,
+        out_shape=pltpu.VMEM((TF * CELLS, NBLK), jnp.float32),
+        in_specs=[far] * 5,
+        out_specs=pl.BlockSpec(memory_space=pltpu.VMEM),
         scratch_shapes=[
+            pltpu.VMEM((CAP, 1, OWNERS), jnp.int32),
+            pltpu.VMEM((CAP, 1, OWNERS), jnp.int32),
+            pltpu.VMEM((1, OWNERS), jnp.int32),
             pltpu.VMEM((TF, CELLS, NBLK), jnp.bfloat16),
             pltpu.VMEM((CAP, CELLS, CELLS, OWNERS), jnp.bfloat16),
             pltpu.VMEM((NBLK, HALF, 2 * CELLS), jnp.float32),
@@ -216,9 +279,13 @@
             pltpu.SMEM((NOCN, 1, OWNERS), jnp.int32),
             pltpu.VMEM((OWNERS, ROWS, 2 * CELLS), jnp.bfloat16),
             pltpu.VMEM((OWNERS, ROWS, 2 * CELLS), jnp.bfloat16),
-            pltpu.SemaphoreType.DMA,
-            pltpu.SemaphoreType.DMA,
-            pltpu.SemaphoreType.DMA,
+            pltpu.VMEM((TF * PAIRS * OWNERS, 2 * CELLS), jnp.float32),
+            pltpu.VMEM((TF * CELLS, 4 * OWNERS), jnp.bfloat16),
+            pltpu.VMEM((PAIRS, 4 * OWNERS, NBLK), jnp.bfloat16),
+            pltpu.SemaphoreType.DMA,
+            pltpu.SemaphoreType.DMA,
+            pltpu.SemaphoreType.DMA,
+            pltpu.SemaphoreType.DMA((3,)),
             pltpu.SemaphoreType.DMA,
             pltpu.SemaphoreType.DMA,
             pltpu.SemaphoreType.DMA,
@@ -230,54 +297,7 @@
             collective_id=0, has_side_effects=True, vmem_limit_bytes=56 << 20
         ),
         name="exchange",
-    )(fields, req, mats)
-
-
-def place_kernel(p_ref, tgt_ref, cnt_ref, o_ref, hot, lhs):
-    @pl.when(pl.program_id(0) == 0)
-    def _():
-        block = lax.broadcasted_iota(jnp.int32, (NBLK, OWNERS), 0)
-        for par in range(2):
-            for p in range(PAIRS):
-                k = 2 * p + par
-                live = jnp.where(cnt_ref[...] > k, tgt_ref[k], -1)
-                at = (par * PAIRS + p) * OWNERS
-                hot[:, at : at + OWNERS] = jnp.where(block == live, 1.0, 0.0).astype(jnp.bfloat16)
-
-    nf = p_ref.shape[0]
-    for f in range(nf):
-        turned = jnp.transpose(p_ref[f])
-        rows = jnp.concatenate([turned[:CELLS], turned[CELLS:]], axis=1)
-        high = rows.astype(jnp.bfloat16)
-        low = (rows - high.astype(jnp.float32)).astype(jnp.bfloat16)
-        lhs[f * CELLS : (f + 1) * CELLS, :] = high
-        lhs[(nf + f) * CELLS : (nf + f + 1) * CELLS, :] = low
-    both = lax.dot_general(
-        lhs[...], hot[...], (((1,), (1,)), ((), ())), preferred_element_type=jnp.float32
-    )
-    total = both[: nf * CELLS] + both[nf * CELLS :]
-    o_ref[...] = total.reshape(nf, CELLS, NBLK)
-
-
-def place(parts, targets, counts):
-    nf = 8
-    return pl.pallas_call(
-        place_kernel,
-        grid=(TF // nf,),
-        out_shape=jax.ShapeDtypeStruct((TF, CELLS, NBLK), jnp.float32),
-        in_specs=[
-            pl.BlockSpec((nf, PAIRS * OWNERS, 2 * CELLS), lambda t: (t, 0, 0)),
-            pl.BlockSpec((CAP, 1, OWNERS), lambda t: (0, 0, 0)),
-            pl.BlockSpec((1, OWNERS), lambda t: (0, 0)),
-        ],
-        out_specs=pl.BlockSpec((nf, CELLS, NBLK), lambda t: (t, 0, 0)),
-        scratch_shapes=[
-            pltpu.VMEM((NBLK, 2 * PAIRS * OWNERS), jnp.bfloat16),
-            pltpu.VMEM((2 * nf * CELLS, 2 * PAIRS * OWNERS), jnp.bfloat16),
-        ],
-        compiler_params=pltpu.CompilerParams(vmem_limit_bytes=48 << 20),
-        name="place",
-    )(parts, targets, counts)
+    )(fields, req, mats, targets, counts)
 
 
 def on_device(atm_fields, requests, ocean_block, live_counts, weights):
@@ -285,8 +305,7 @@
     req = jnp.transpose(requests, (2, 0, 1))
     targets = jnp.transpose(ocean_block, (2, 0, 1))
     mats = jnp.transpose(weights[0], (1, 2, 3, 0))
-    parts = exchange(fields, req, mats)
-    out = place(parts.reshape(TF, PAIRS * OWNERS, 2 * CELLS), targets, live_counts)
+    out = exchange(fields, req, mats, targets, live_counts)
     return jnp.transpose(out.reshape(4, 8, CELLS, NBLK), (3, 0, 1, 2))
 
 

time: 69.4 us -> 65.3 us (0.941)
  Pallas kernels: 69.2 us -> 63.2 us
  local copies, waits for them, and re-layouts: 0.01 us -> 2.02 us
    pallas_call x2 -> x1, Pallas kernels: 69.2 us -> 63.2 us  [exchange(): pl.pallas_call(exchange_kernel, out_shape=pltpu.VMEM((TF * CELLS, NBLK),...]
    unnamed x4 -> x1, local copies, waits for them, and re-layouts: 0.01 us -> 2.02 us
where the time goes in v3:
time: 65.3 us; the launch traced here: 65.2 us
  Pallas kernels  63.2 us (97%)
  local copies, waits for them, and re-layouts  2.02 us (3%)
    pallas_call x1, Pallas kernels, exchange(): pl.pallas_call(exchange_kernel, out_shape=pltpu.VMEM((TF * CELLS, NBLK),...  63.2 us
    unnamed x1, local copies, waits for them, and re-layouts  2.02 us

profile of v3, /device:TPU:8, one launch (start us, length us, event | category | flops | bytes accessed | tf_op | source)
XLA Modules:
  0.0 65.2 jit_solution(11439728576807644989)
XLA Ops:
  0.0 63.2 %exchange.1 = f32[2048,512]{1,0:T(8,128)S(1)} custom-call(bf16[32,64,512]{2,1,0:T(8,128)(2,1)} %bitcast.13, s32[6,1,128]{2,1,0:T(1,128)} %bitcast.14, bf16[6,64,64,128]{3,2,1,0:T(8,128)(2,1)} %bitcast.12, s32[6,1,128]{2,1,0:T(1,128)} %bitcast.15, s32[1,128]{1,0:T(1,128)} %cnt_hbm.1), custom_call_target="tpu_custom_call" | custom-call | tf_op jit(solution)/shard_map/exchange/pallas_call | solution.py:261
  63.2 2.0 %copy.7 = f32[512,4,8,64]{0,3,2,1:T(8,128)} copy(f32[512,4,8,64]{0,3,2,1:T(8,128)S(1)} %bitcast.11) | data formatting | bytes 8388608

commit v4 on v3

--- a/solution.py
+++ b/solution.py
@@ -17,14 +17,14 @@
 HALF = 16
 NBLK = 512
 GROUPS = 16
-TFS = 16
+TFS = 32
 PER = OWNERS // GROUPS
 ROWS = PAIRS * TF
 WPITCH = CELLS
 
 
 def shift_of(i):
-    j = (i * 37) % OWNERS
+    j = (i * 59) % OWNERS
     return j // 32, (j // 16) % 2, (j // 4) % 4, j % 4
 
 
@@ -42,7 +42,7 @@
 def sender_of(i):
     atm = lax.axis_index("atm")
     ocn = lax.axis_index("ocn")
-    j = (i * 37) & (OWNERS - 1)
+    j = (i * 59) & (OWNERS - 1)
     y = (atm // 2 - (j >> 5)) & 3
     c = (atm % 2 - (j >> 4)) & 1
     x = (ocn // 4 - (j >> 2)) & 3
@@ -239,7 +239,7 @@
             send.at[pl.ds(0, n)], recv.at[pl.ds(0, n)], dsend, drecv.at[g],
             device_id=(atm, ocn), device_id_type=MESH,
         ).wait_recv()
-        lax.fori_loop(g * PER, (g + 1) * PER, apply, 0, unroll=4)
+        lax.fori_loop(g * PER, (g + 1) * PER, apply, 0, unroll=8)
         for b in range(PAIRS):
             if g * PER * PAIRS < (b + 1) * OWNERS <= (g + 1) * PER * PAIRS:
                 def some(q, carry):

time: 65.3 us -> 58.8 us (0.900)
  the two profiles are of different devices: /device:TPU:8 before, /device:TPU:1 now
where the time goes in v4:
time: 58.8 us; the launch traced here: 58.7 us
  Pallas kernels  56.6 us (96%)
  local copies, waits for them, and re-layouts  2.02 us (3%)
    pallas_call x1, Pallas kernels, exchange(): pl.pallas_call(exchange_kernel, out_shape=pltpu.VMEM((TF * CELLS, NBLK),...  56.6 us
    unnamed x1, local copies, waits for them, and re-layouts  2.02 us

profile of v4, /device:TPU:1, one launch (start us, length us, event | category | flops | bytes accessed | tf_op | source)
XLA Modules:
  0.0 58.7 jit_solution(215204005221152861)
XLA Ops:
  0.0 56.6 %exchange.1 = f32[2048,512]{1,0:T(8,128)S(1)} custom-call(bf16[32,64,512]{2,1,0:T(8,128)(2,1)} %bitcast.13, s32[6,1,128]{2,1,0:T(1,128)} %bitcast.14, bf16[6,64,64,128]{3,2,1,0:T(8,128)(2,1)} %bitcast.12, s32[6,1,128]{2,1,0:T(1,128)} %bitcast.15, s32[1,128]{1,0:T(1,128)} %cnt_hbm.1), custom_call_target="tpu_custom_call" | custom-call | tf_op jit(solution)/shard_map/exchange/pallas_call | solution.py:261
  56.6 2.0 %copy.7 = f32[512,4,8,64]{0,3,2,1:T(8,128)} copy(f32[512,4,8,64]{0,3,2,1:T(8,128)S(1)} %bitcast.11) | data formatting | bytes 8388608

commit v5 on v4

--- a/solution.py
+++ b/solution.py
@@ -17,14 +17,13 @@
 HALF = 16
 NBLK = 512
 GROUPS = 16
-TFS = 32
 PER = OWNERS // GROUPS
 ROWS = PAIRS * TF
 WPITCH = CELLS
 
 
 def shift_of(i):
-    j = (i * 59) % OWNERS
+    j = (i * 91) % OWNERS
     return j // 32, (j // 16) % 2, (j // 4) % 4, j % 4
 
 
@@ -42,7 +41,7 @@
 def sender_of(i):
     atm = lax.axis_index("atm")
     ocn = lax.axis_index("ocn")
-    j = (i * 59) & (OWNERS - 1)
+    j = (i * 91) & (OWNERS - 1)
     y = (atm // 2 - (j >> 5)) & 3
     c = (atm % 2 - (j >> 4)) & 1
     x = (ocn // 4 - (j >> 2)) & 3
@@ -199,8 +198,13 @@
             mine = goal[b * OWNERS : (b + 1) * OWNERS]
             ones = jnp.where(block == mine, 1.0, 0.0).astype(jnp.bfloat16)
             for h in range(2):
-                at = (2 * h + par) * OWNERS
-                hot[b, at : at + OWNERS, :] = ones
+                if b < PAIRS - 1:
+                    at = (2 * h + par) * OWNERS
+                    hot[b, at : at + OWNERS, :] = ones
+                    continue
+                for u in range(2):
+                    at = u * 2 * OWNERS + (2 * par + h) * CELLS
+                    hot[b, at : at + CELLS, :] = ones[u * CELLS : (u + 1) * CELLS]
 
     lane = lax.broadcasted_iota(jnp.int32, (CELLS, 2 * CELLS), 1) < CELLS
 
@@ -217,22 +221,42 @@
         return carry
 
     def turn_parts(b, tf):
-        rows = part[pl.ds(pl.multiple_of(tf * PAIRS * OWNERS + b * OWNERS, OWNERS), OWNERS), :]
+        rows = part[pl.ds(tf * PAIRS * OWNERS + b * OWNERS, OWNERS), :]
         rows = jnp.transpose(rows)
         high = rows.astype(jnp.bfloat16)
         low = (rows - high.astype(jnp.float32)).astype(jnp.bfloat16)
-        at = pl.ds(pl.multiple_of(tf * CELLS, CELLS), CELLS)
+        at = pl.ds(tf * CELLS, CELLS)
         for h, term in enumerate((high, low)):
             lhs[at, 2 * h * OWNERS : (2 * h + 1) * OWNERS] = term[:CELLS]
             lhs[at, (2 * h + 1) * OWNERS : (2 * h + 2) * OWNERS] = term[CELLS:]
 
-    def place(b, tf):
-        at = pl.ds(pl.multiple_of(tf * CELLS, CELLS), TFS * CELLS)
-        more = jnp.dot(lhs[at, :], hot[b], preferred_element_type=jnp.float32)
-        if b:
-            more += acc[at, :]
-        acc[at, :] = more
-
+    def turn_half(u, tf):
+        first = (PAIRS - 1) * OWNERS + u * CELLS
+        rows = part[pl.ds(tf * PAIRS * OWNERS + first, CELLS), :]
+        high = rows.astype(jnp.bfloat16).astype(jnp.float32)
+        both = jnp.transpose(jnp.concatenate([high, rows - high], axis=0)).astype(jnp.bfloat16)
+        at = pl.ds(tf * CELLS, CELLS)
+        lhs[at, :OWNERS] = both[:CELLS]
+        lhs[at, OWNERS : 2 * OWNERS] = both[CELLS:]
+
+    def place(n):
+        for t in range(TF):
+            if n < PAIRS - 1:
+                turn_parts(n, t)
+            else:
+                turn_half(n - PAIRS + 1, t)
+        if n < PAIRS - 1:
+            more = jnp.dot(lhs[...], hot[n], preferred_element_type=jnp.float32)
+        else:
+            at = (n - PAIRS + 1) * 2 * OWNERS
+            more = jnp.dot(
+                lhs[:, : 2 * OWNERS], hot[PAIRS - 1, at : at + 2 * OWNERS, :],
+                preferred_element_type=jnp.float32,
+            )
+        acc[...] = more if n == 0 else acc[...] + more
+
+    ready = [(b + 1) * OWNERS for b in range(PAIRS - 1)]
+    ready += [PAIRS * OWNERS - CELLS, PAIRS * OWNERS]
     for g in range(GROUPS):
         n = PER - 1 if g == 0 else PER
         pltpu.make_async_remote_copy(
@@ -240,15 +264,9 @@
             device_id=(atm, ocn), device_id_type=MESH,
         ).wait_recv()
         lax.fori_loop(g * PER, (g + 1) * PER, apply, 0, unroll=8)
-        for b in range(PAIRS):
-            if g * PER * PAIRS < (b + 1) * OWNERS <= (g + 1) * PER * PAIRS:
-                def some(q, carry):
-                    for t in range(TFS):
-                        turn_parts(b, q * TFS + t)
-                    place(b, q * TFS)
-                    return carry
-
-                lax.fori_loop(0, TF // TFS, some, 0)
+        for n, bound in enumerate(ready):
+            if g * PER * PAIRS < bound <= (g + 1) * PER * PAIRS:
+                place(n)
 
     pltpu.make_async_remote_copy(
         send.at[pl.ds(1, OWNERS - 1)], recv.at[pl.ds(1, OWNERS - 1)], dsend, drecv.at[0],

time: 58.8 us -> 58.1 us (0.988)
  Pallas kernels: 56.6 us -> 56 us
    pallas_call x1, Pallas kernels: 56.6 us -> 56 us  [exchange(): pl.pallas_call(exchange_kernel, out_shape=pltpu.VMEM((TF * CELLS, NBLK),...]
where the time goes in v5:
time: 58.1 us; the launch traced here: 58 us
  Pallas kernels  56 us (96%)
  local copies, waits for them, and re-layouts  2.02 us (3%)
    pallas_call x1, Pallas kernels, exchange(): pl.pallas_call(exchange_kernel, out_shape=pltpu.VMEM((TF * CELLS, NBLK),...  56 us
    unnamed x1, local copies, waits for them, and re-layouts  2.02 us

profile of v5, /device:TPU:1, one launch (start us, length us, event | category | flops | bytes accessed | tf_op | source)
XLA Modules:
  0.0 58.0 jit_solution(13480083924659152564)
XLA Ops:
  0.0 56.0 %exchange.1 = f32[2048,512]{1,0:T(8,128)S(1)} custom-call(bf16[32,64,512]{2,1,0:T(8,128)(2,1)} %bitcast.13, s32[6,1,128]{2,1,0:T(1,128)} %bitcast.14, bf16[6,64,64,128]{3,2,1,0:T(8,128)(2,1)} %bitcast.12, s32[6,1,128]{2,1,0:T(1,128)} %bitcast.15, s32[1,128]{1,0:T(1,128)} %cnt_hbm.1), custom_call_target="tpu_custom_call" | custom-call | tf_op jit(solution)/shard_map/exchange/pallas_call | solution.py:279
  56.0 2.0 %copy.7 = f32[512,4,8,64]{0,3,2,1:T(8,128)} copy(f32[512,4,8,64]{0,3,2,1:T(8,128)S(1)} %bitcast.11) | data formatting | bytes 8388608

commit v6 on v5

--- a/solution.py
+++ b/solution.py
@@ -16,7 +16,7 @@
 TF = 32
 HALF = 16
 NBLK = 512
-GROUPS = 16
+GROUPS = 32
 PER = OWNERS // GROUPS
 ROWS = PAIRS * TF
 WPITCH = CELLS
@@ -263,7 +263,7 @@
             send.at[pl.ds(0, n)], recv.at[pl.ds(0, n)], dsend, drecv.at[g],
             device_id=(atm, ocn), device_id_type=MESH,
         ).wait_recv()
-        lax.fori_loop(g * PER, (g + 1) * PER, apply, 0, unroll=8)
+        lax.fori_loop(g * PER, (g + 1) * PER, apply, 0, unroll=4)
         for n, bound in enumerate(ready):
             if g * PER * PAIRS < bound <= (g + 1) * PER * PAIRS:
                 place(n)

time: 58.1 us -> 58.3 us (level)
  no operation moved by 1% of the time
where the time goes in v6:
time: 58.3 us; the launch traced here: 58.2 us
  Pallas kernels  56.2 us (96%)
  local copies, waits for them, and re-layouts  2.02 us (3%)
    pallas_call x1, Pallas kernels, exchange(): pl.pallas_call(exchange_kernel, out_shape=pltpu.VMEM((TF * CELLS, NBLK),...  56.2 us
    unnamed x1, local copies, waits for them, and re-layouts  2.02 us

profile of v6, /device:TPU:1, one launch (start us, length us, event | category | flops | bytes accessed | tf_op | source)
XLA Modules:
  0.0 58.2 jit_solution(2386977859427287067)
XLA Ops:
  0.0 56.2 %exchange.1 = f32[2048,512]{1,0:T(8,128)S(1)} custom-call(bf16[32,64,512]{2,1,0:T(8,128)(2,1)} %bitcast.13, s32[6,1,128]{2,1,0:T(1,128)} %bitcast.14, bf16[6,64,64,128]{3,2,1,0:T(8,128)(2,1)} %bitcast.12, s32[6,1,128]{2,1,0:T(1,128)} %bitcast.15, s32[1,128]{1,0:T(1,128)} %cnt_hbm.1), custom_call_target="tpu_custom_call" | custom-call | tf_op jit(solution)/shard_map/exchange/pallas_call | solution.py:279
  56.2 2.0 %copy.7 = f32[512,4,8,64]{0,3,2,1:T(8,128)} copy(f32[512,4,8,64]{0,3,2,1:T(8,128)S(1)} %bitcast.11) | data formatting | bytes 8388608
